TPU v7x, 32 devices: a whole 2x2x4 slice. The times are simulated.
32 devices in a mesh: vec: 16 (over z, y, x), orb: 2 (over core).
Axes of the slice: x: 2, y: 2, z: 4, core: 2. Of those that a mesh axis runs over, the one named last changes fastest.
Arguments:
- cholesky: bfloat16 [64, 2048, 2048], P('vec', 'orb'), may hold values from -4 to 4
- active_coeff: bfloat16 [2048, 24], replicated, may hold values from -0.125 to 0.125
- pair_density: bfloat16 [24, 24, 576], replicated, may hold values from -0.0546875 to 0.0546875
Outputs:
- active_integrals: float32 [2048, 24, 576], P(('orb', 'vec'))
- general_fock: float32 [2048, 24], P(('orb', 'vec'))
All inputs are finite; a program needn't handle non-finite values.
Results may differ from a plain program's by a relative error of at most 0.0049.
Values may be sent and summed in bfloat16 or wider, within the bound.
No kernel may reach another device: no remote copies, remote signals or barrier semaphores. Data moves between devices by JAX's collectives and lax.ppermute only.
A program may use at most 64 MiB of HBM per device.

v0:
```python
import jax
import jax.numpy as jnp
from jax import lax
from jax.sharding import PartitionSpec as P


def shards(cholesky, active_coeff, pair_density):
    vec_count = lax.axis_size("vec")
    orb_pos = lax.axis_index("orb")
    local_vecs, block_rows, basis = cholesky.shape
    n_act = active_coeff.shape[1]
    rows_here = block_rows // vec_count
    half = jnp.einsum(
        "qmn,nu->mqu", cholesky, active_coeff, preferred_element_type=jnp.float32
    ).astype(jnp.bfloat16)
    flat = half.reshape(block_rows, local_vecs * n_act)
    moved = lax.all_to_all(flat, "vec", split_axis=0, concat_axis=1, tiled=True)
    regrouped = moved.reshape(rows_here, -1, n_act)
    coeff_rows = lax.dynamic_slice_in_dim(active_coeff, orb_pos * block_rows, block_rows, 0)
    partial_value = jnp.einsum("mv,mqw->qvw", coeff_rows, half, preferred_element_type=jnp.float32)
    own_sum = lax.psum(partial_value.reshape(local_vecs, n_act * n_act), "orb")
    own_active = own_sum.astype(jnp.bfloat16)
    integrals = jnp.einsum(
        "mqu,qx->mux",
        regrouped,
        lax.all_gather(own_active, "vec", axis=0, tiled=True),
        preferred_element_type=jnp.float32,
    )
    density = pair_density.astype(jnp.float32)
    fock = jnp.dot(
        integrals.reshape(rows_here, -1),
        density.reshape(n_act, -1).T,
        precision=lax.Precision.HIGHEST,
    )
    return (integrals, fock)


def solution(mesh):
    return jax.shard_map(
        shards,
        mesh=mesh,
        in_specs=(P("vec", "orb", None), P(), P()),
        out_specs=(P(("orb", "vec"), None, None), P(("orb", "vec"), None)),
        check_vma=False,
    )
```

profile of v0, /device:TPU:0, one launch (start us, length us, event | category | flops | bytes accessed | tf_op | source)
XLA Modules:
  0.0 70.2 jit_solution(7245884175089392556)
XLA Ops:
  0.6 0.0 copy-start
  0.6 0.0 copy-start.2
  0.7 10.4 %fusion.2 = bf16[1024,4,24]{0,2,1:T(8,128)(2,1)S(1)} fusion(bf16[4,1024,2048]{2,1,0:T(8,128)(2,1)} %param.3, bf16[2048,24]{0,1:T(8,128)(2,1)} %param.4), kind=kOutput, calls=%fused_computation.3 | convolution fusion | flops 402751488 | bytes 17072128 | tf_op jit(solution)/shard_map/qmn,nu->mqu/dot_general | solution.py:13
  11.0 0.3 all_to_all.12
  11.3 1.1 %copy.12 = bf16[16,64,96]{2,1,0:T(8,128)(2,1)} copy(bf16[16,64,96]{1,0,2:T(8,128)(2,1)S(1)} %all_to_all.12) | data formatting | bytes 393216 | tf_op jit(solution)/shard_map/all_to_all | solution.py:17
  12.4 8.3 %all-to-all-start = ((bf16[16,64,96]{2,1,0:T(8,128)(2,1)}), bf16[16,64,96]{2,1,0:T(8,128)(2,1)S(1)}, u32[]{:S(2)}, u32[]{:S(2)}) async-start(bf16[16,64,96]{2,1,0:T(8,128)(2,1)} %copy.12), calls=%async_computation | async-start | bytes 524288 | tf_op jit(solution)/shard_map/all_to_all | solution.py:17
  20.7 0.0 copy-done.2
  20.7 0.2 convolution_bitcast_fusion
  20.9 0.1 copy.14
  21.0 0.1 reshape.19
  21.1 3.3 %psum.7 = bf16[4,576]{1,0:T(4,128)(2,1)S(1)} all-reduce(f32[4,576]{1,0:T(4,128)S(1)} %reshape.19), channel_id=1, replica_groups=mesh['vec'=16,'orb'=2] {'orb'}, use_global_device_ids=true, to_apply=%region_0.0 | all-reduce | flops 2304 | bytes 13824 | tf_op jit(solution)/shard_map/psum | solution.py:21
  24.4 41.4 %all-gather = bf16[16,4,576]{2,1,0:T(4,128)(2,1)S(1)} all-gather(bf16[1,4,576]{2,1,0:T(4,128)(2,1)S(1)} %bitcast.25), channel_id=1, replica_groups=mesh['vec'=16,'orb'=2] {'vec'}, dimensions={0}, use_global_device_ids=true | all-gather | bytes 78336 | tf_op jit(solution)/shard_map/all_gather | solution.py:26
  65.8 0.0 all-to-all-done
  65.8 0.2 copy.13
  66.0 0.4 copy.15
  66.4 0.8 %fusion.11 = f32[64,24,576]{2,1,0:T(8,128)S(1)} fusion(bf16[64,64,24]{1,2,0:T(8,128)(2,1)S(1)} %copy.15, bf16[64,576,1]{1,0,2:T(8,128)(2,1)S(1)} %reshape.24), kind=kOutput, calls=%fused_computation.12 | convolution fusion | flops 113246208 | bytes 3809280 | tf_op jit(solution)/shard_map/mqu,qx->mux/dot_general | solution.py:23
  67.2 0.0 copy-done
  67.2 0.0 copy-start.1
  67.2 2.9 %fusion.3 = f32[64,24]{0,1:T(8,128)} fusion(f32[64,24,576]{2,1,0:T(8,128)S(1)} %fusion.11, bf16[24,24,576]{2,1,0:T(8,128)(2,1)S(1)} %copy-done), kind=kOutput, calls=%fused_computation.5 | convolution fusion | flops 254803968 | bytes 4208640 | tf_op jit(solution)/shard_map/dot_general | solution.py:30
  70.2 0.0 copy-done.1
  (1 shorter events, 0.0 us)
Async XLA Ops:
  0.6 66.6 %copy-start = (bf16[24,24,576]{2,1,0:T(8,128)(2,1)S(1)}, bf16[24,24,576]{2,1,0:T(8,128)(2,1)}, u32[]{:S(2)}) copy-start(bf16[24,24,576]{2,1,0:T(8,128)(2,1)} %param.5) | copy-start | bytes 1990660
  0.6 20.1 %copy-start.2 = (bf16[2048,24]{0,1:T(8,128)(2,1)S(1)}, bf16[2048,24]{0,1:T(8,128)(2,1)}, u32[]{:S(2)}) copy-start(bf16[2048,24]{0,1:T(8,128)(2,1)} %param.4) | copy-start | bytes 294916
  12.4 53.4 %all-to-all-start = ((bf16[16,64,96]{2,1,0:T(8,128)(2,1)}), bf16[16,64,96]{2,1,0:T(8,128)(2,1)S(1)}, u32[]{:S(2)}, u32[]{:S(2)}) async-start(bf16[16,64,96]{2,1,0:T(8,128)(2,1)} %copy.12), calls=%async_computation | async-start | bytes 524288 | tf_op jit(solution)/shard_map/all_to_all | solution.py:17
  67.2 2.9 %copy-start.1 = (f32[64,24,576]{2,1,0:T(8,128)}, f32[64,24,576]{2,1,0:T(8,128)S(1)}, u32[]{:S(2)}) copy-start(f32[64,24,576]{2,1,0:T(8,128)S(1)} %fusion.11) | copy-start | bytes 10616836
where the time goes:
time: 70.4 us; the launch traced here: 70.2 us
  blocking collectives  44.7 us (63%)
  matrix products  14.3 us (20%)
  starting transfers between devices  8.31 us (12%)
  local copies, waits for them, and re-layouts  2.18 us (3%)
  between operations  0.73 us (1%)
    all_gather x1, blocking collectives, shards(): lax.all_gather(own_active, 'vec', axis=0, tiled=True)  41.4 us
    dot_general x1, matrix products, shards(): jnp.einsum('qmn,nu->mqu', cholesky, active_coeff, preferred_element_type=...  10.4 us
    all_to_all x1, starting transfers between devices, shards(): moved = lax.all_to_all(flat, 'vec', split_axis=0, concat_axis=1, tiled=True)  8.31 us
    psum x1, blocking collectives, shards(): own_sum = lax.psum(partial_value.reshape(local_vecs, n_act * n_act), 'orb')  3.3 us
    dot_general x1, matrix products, shards(): jnp.dot(integrals.reshape(rows_here, -1), density.reshape(n_act, -1).T, p...  2.92 us
    all_to_all x3, local copies, waits for them, and re-layouts, shards(): moved = lax.all_to_all(flat, 'vec', split_axis=0, concat_axis=1, tiled=True)  1.57 us
  transfers between devices with their start and end apart: 1, of which 0 were waited for; matrix products, arithmetic and copies ran while one was open for 1% of the time, Pallas kernels for 0%

commit v1 on v0

v1 whole, which is shorter than its diff:
```python
import functools

import jax
import jax.numpy as jnp
from jax import lax
from jax.experimental import pallas as pl
from jax.experimental.pallas import tpu as pltpu
from jax.sharding import PartitionSpec as P

LANES = 128
SUBLANES = 8
BF16 = jnp.bfloat16
F32 = jnp.float32


def transform_kernel(orb_ref, chol_ref, coeff_hbm, half_ref, partial_ref, rows_buf, coeff_row, sems, coeff_sem):
    n_act = coeff_hbm.shape[0]
    rows_all = chol_ref.shape[0]
    block_rows = half_ref.shape[0] * LANES
    size = block_rows // 2
    small = size // 2
    bigs = rows_all // size

    def copy(start, count, sem):
        rows = pl.ds(start, count)
        return pltpu.make_async_copy(chol_ref.at[rows], rows_buf.at[rows], sem)

    def small_copy(i):
        return copy(pl.multiple_of(i * small, small), small, sems.at[i])

    def big_copy(i):
        return copy(pl.multiple_of(i * size, size), size, sems.at[i + 1])

    def step(start, count):
        value = lax.dot_general(
            coeff_row[...],
            rows_buf[pl.ds(start, count), :],
            (((1,), (1,)), ((), ())),
            preferred_element_type=F32,
        )
        rows = pl.ds(pl.multiple_of(lax.div(start, block_rows) * n_act, n_act), n_act)
        tile = lax.div(lax.rem(start, block_rows), LANES)
        value = value.astype(BF16).astype(F32)
        for i in range(count // LANES):
            half_ref[tile + i, rows, :] = value[:, i * LANES:(i + 1) * LANES]

    coeff_copy = pltpu.make_async_copy(coeff_hbm, coeff_row, coeff_sem)
    coeff_copy.start()

    @pl.loop(0, 2)
    def _(i):
        small_copy(i).start()

    @pl.loop(1, bigs)
    def _(i):
        big_copy(i).start()

    coeff_copy.wait()

    @pl.loop(0, 2)
    def _(i):
        small_copy(i).wait()
        step(pl.multiple_of(i * small, small), small)

    @pl.loop(1, bigs)
    def _(i):
        big_copy(i).wait()
        step(pl.multiple_of(i * size, size), size)

    own = pl.multiple_of(orb_ref[0] * block_rows, block_rows)
    partial_ref[...] = lax.dot_general(
        coeff_row[:, pl.ds(own, block_rows)],
        jnp.concatenate([half_ref[i] for i in range(half_ref.shape[0])], axis=1).astype(BF16),
        (((1,), (1,)), ((), ())),
        preferred_element_type=F32,
    )


def transform(cholesky, coeff_t, orb_pos):
    vecs, block_rows, basis = cholesky.shape
    n_act = coeff_t.shape[0]
    width = vecs * n_act
    flat = cholesky.reshape(vecs * block_rows, basis)
    return pl.pallas_call(
        transform_kernel,
        out_shape=(
            jax.ShapeDtypeStruct((block_rows // LANES, width, LANES), F32),
            jax.ShapeDtypeStruct((n_act, width), F32),
        ),
        in_specs=[
            pl.BlockSpec(memory_space=pltpu.SMEM),
            pl.BlockSpec(memory_space=pltpu.HBM),
            pl.BlockSpec(memory_space=pltpu.HBM),
        ],
        out_specs=(pl.BlockSpec(memory_space=pltpu.VMEM),) * 2,
        scratch_shapes=[
            pltpu.VMEM(flat.shape, BF16),
            pltpu.VMEM((n_act, basis), BF16),
            pltpu.SemaphoreType.DMA((2 * vecs + 1,)),
            pltpu.SemaphoreType.DMA,
        ],
        compiler_params=pltpu.CompilerParams(vmem_limit_bytes=40 * 2**20),
        cost_estimate=pl.CostEstimate(
            flops=2 * vecs * block_rows * basis * 256,
            bytes_accessed=2 * vecs * block_rows * basis,
            transcendentals=0,
        ),
    )(
        orb_pos[None],
        pltpu.with_memory_space_constraint(flat, pltpu.HBM),
        pltpu.with_memory_space_constraint(coeff_t, pltpu.HBM),
    )


def reverse(index, count):
    result = 0
    while count > 1:
        result = 2 * result + index % 2
        index //= 2
        count //= 2
    return result


def chunk_kernel(vecs, half_ref, packed_ref, turned):
    tiles, width, _ = half_ref.shape
    groups = width // SUBLANES
    span = LANES // SUBLANES
    shape = (groups, SUBLANES, LANES)
    row = lax.broadcasted_iota(jnp.int32, shape, 1)
    block = lax.broadcasted_iota(jnp.int32, shape, 2) // span
    source = lax.broadcasted_iota(jnp.int32, (LANES, LANES), 0)
    target = lax.broadcasted_iota(jnp.int32, (LANES, LANES), 1)
    order = jnp.where(source == target % SUBLANES * span + target // SUBLANES, 1.0, 0.0).astype(BF16)
    for tile in range(tiles):
        value = half_ref[tile].reshape(shape)
        for step in (1, 2, 4):
            up = pltpu.roll(pltpu.roll(value, SUBLANES - step, 1), step * span, 2)
            down = pltpu.roll(pltpu.roll(value, step, 1), LANES - step * span, 2)
            swapped = jnp.where(row & step == 0, up, down)
            value = jnp.where((row & step) == (block & step), value, swapped)
        value = jnp.dot(value.reshape(width, LANES).astype(BF16), order, preferred_element_type=F32)
        turned[tile] = value
        per_vec = width // vecs
        half = SUBLANES // 2
        for d in range(2):
            place = reverse(2 * tile + d, 2 * tiles)
            for t in range(per_vec // 2):
                at = t // half * SUBLANES + d * half + t % half
                part = turned[tile, pl.ds(at, vecs, stride=per_vec), :]
                packed_ref[place, :, t * LANES:(t + 1) * LANES] = part.astype(BF16)


def split(half, vecs):
    tiles, width, _ = half.shape
    n_act = width // vecs
    lanes = n_act // 2 * LANES + -(-n_act * n_act // LANES) * LANES
    return pl.pallas_call(
        functools.partial(chunk_kernel, vecs),
        out_shape=jax.ShapeDtypeStruct((2 * tiles, vecs, lanes), BF16),
        in_specs=[pl.BlockSpec(memory_space=pltpu.VMEM)],
        out_specs=pl.BlockSpec(memory_space=pltpu.VMEM),
        scratch_shapes=[pltpu.VMEM(half.shape, F32)],
        compiler_params=pltpu.CompilerParams(vmem_limit_bytes=4 * 2**20),
        cost_estimate=pl.CostEstimate(flops=0, bytes_accessed=2**20, transcendentals=0),
    )(half)


def pack_kernel(vecs, n_act, packed_in, own_ref, other_ref, packed_ref):
    chunks, _, lanes = packed_ref.shape
    first = n_act // 2 * LANES
    total = (own_ref[...] + other_ref[...]).astype(BF16).astype(F32)
    tall = jnp.concatenate([total[:, q * n_act:(q + 1) * n_act] for q in range(vecs)], axis=0)
    shape = (n_act, lanes - first)
    place = lax.broadcasted_iota(jnp.int32, shape, 0)
    lane = lax.broadcasted_iota(jnp.int32, shape, 1)
    spread = jnp.where(lane % n_act == place, 1.0, 0.0).astype(BF16)
    wide = jnp.dot(tall.astype(BF16), spread, preferred_element_type=F32)
    picked = jnp.where(lane // n_act == place, 1.0, 0.0)
    flat = jnp.concatenate(
        [
            jnp.sum(wide[q * n_act:(q + 1) * n_act] * picked, axis=0, keepdims=True)
            for q in range(vecs)
        ],
        axis=0,
    )
    tail = flat.astype(BF16)
    for c in range(chunks):
        packed_ref[c, :, :first] = packed_in[c, :, :first]
        packed_ref[c, :, first:] = tail


def pack(packed, own, other, vecs, n_act):
    return pl.pallas_call(
        functools.partial(pack_kernel, vecs, n_act),
        out_shape=jax.ShapeDtypeStruct(packed.shape, BF16),
        in_specs=[pl.BlockSpec(memory_space=pltpu.VMEM)] * 3,
        out_specs=pl.BlockSpec(memory_space=pltpu.VMEM),
        compiler_params=pltpu.CompilerParams(vmem_limit_bytes=4 * 2**20),
        cost_estimate=pl.CostEstimate(flops=0, bytes_accessed=2**18, transcendentals=0),
    )(packed, own, other)


def finish_kernel(vecs, n_act, moved_ref, density_hbm, out_hbm, fock_ref, wide, left, active, stack, density, folded, weights, out_buf, sems, density_sem):
    sources = moved_ref.shape[0]
    rows_here = LANES // 2
    pairs = n_act * n_act
    total = sources * vecs
    groups = n_act // SUBLANES
    span = LANES // SUBLANES
    parts = rows_here // span
    density_copy = pltpu.make_async_copy(density_hbm, density, density_sem)
    density_copy.start()

    def collect(t):
        for s in range(sources):
            part = moved_ref[s, :, t * LANES:(t + 1) * LANES].astype(F32)
            wide[t, s * vecs:(s + 1) * vecs, :] = part
        return wide[t].astype(BF16)

    for j in range(active.shape[1] // LANES):
        active[:, j * LANES:(j + 1) * LANES] = collect(groups * parts + j)
    def arrange(g):
        for p in range(parts):
            value = collect(g * parts + p)
            cols = slice(p * LANES, (p + 1) * LANES)
            stack[g * total:(g + 1) * total, cols] = value
            left[g, cols] = value.T

    copies = []
    arrange(0)
    for g in range(groups):
        value = jnp.dot(left[g], active[:, :pairs], preferred_element_type=F32)
        if g + 1 < groups:
            arrange(g + 1)
        out_buf[g] = value.reshape(rows_here, SUBLANES, pairs)
        copies.append(
            pltpu.make_async_copy(
                out_buf.at[g], out_hbm.at[:, pl.ds(g * SUBLANES, SUBLANES), :], sems.at[g]
            )
        )
        copies[-1].start()
    density_copy.wait()
    folded[:, :total] = lax.dot_general(
        density[...], active[:, :pairs], (((1,), (1,)), ((), ())), preferred_element_type=F32
    )
    for u in range(n_act):
        value = folded[pl.ds(u, n_act, stride=n_act), :][:, :total]
        high = value.astype(BF16).astype(F32)
        rows = slice(u % SUBLANES * n_act, (u % SUBLANES + 1) * n_act)
        cols = slice(u // SUBLANES * total, (u // SUBLANES + 1) * total)
        weights[0, rows, cols] = high
        weights[1, rows, cols] = value - high
    both = weights[...].reshape(2 * SUBLANES * n_act, groups * total).astype(BF16)
    both = jnp.dot(both, stack[...], preferred_element_type=F32)
    sums = both[:SUBLANES * n_act] + both[SUBLANES * n_act:]
    lane = lax.broadcasted_iota(jnp.int32, (n_act, rows_here * SUBLANES), 1) % SUBLANES
    rest = sums[:n_act]
    for u in range(1, SUBLANES):
        rest = jnp.where(lane == u, sums[u * n_act:(u + 1) * n_act], rest)
    shape = (rows_here * SUBLANES, rows_here)
    member = lax.broadcasted_iota(jnp.int32, shape, 0) // SUBLANES
    member = jnp.where(member == lax.broadcasted_iota(jnp.int32, shape, 1), 1.0, 0.0).astype(BF16)
    result = jnp.zeros((n_act, rows_here), F32)
    for _ in range(2):
        piece = rest.astype(BF16)
        rest = rest - piece.astype(F32)
        result += jnp.dot(piece, member, preferred_element_type=F32)
    fock_ref[...] = result
    for each in copies:
        each.wait()


def finish(moved, density, vecs, n_act):
    sources, _, lanes = moved.shape
    rows_here = LANES // 2
    total = sources * vecs
    pairs = n_act * n_act
    groups = n_act // SUBLANES
    padded = -(-pairs // LANES) * LANES
    return pl.pallas_call(
        functools.partial(finish_kernel, vecs, n_act),
        out_shape=(
            jax.ShapeDtypeStruct((rows_here, n_act, pairs), F32),
            jax.ShapeDtypeStruct((n_act, rows_here), F32),
        ),
        in_specs=[
            pl.BlockSpec(memory_space=pltpu.VMEM),
            pl.BlockSpec(memory_space=pltpu.HBM),
        ],
        out_specs=(pl.BlockSpec(memory_space=pl.ANY), pl.BlockSpec(memory_space=pltpu.VMEM)),
        scratch_shapes=[
            pltpu.VMEM((lanes // LANES, total, LANES), F32),
            pltpu.VMEM((groups, rows_here * SUBLANES, total), BF16),
            pltpu.VMEM((total, padded), BF16),
            pltpu.VMEM((groups * total, rows_here * SUBLANES), BF16),
            pltpu.VMEM((pairs, pairs), BF16),
            pltpu.VMEM((pairs, LANES), F32),
            pltpu.VMEM((2, SUBLANES * n_act, groups * total), F32),
            pltpu.VMEM((groups, rows_here, SUBLANES, pairs), F32),
            pltpu.SemaphoreType.DMA((groups,)),
            pltpu.SemaphoreType.DMA,
        ],
        compiler_params=pltpu.CompilerParams(vmem_limit_bytes=16 * 2**20),
        cost_estimate=pl.CostEstimate(
            flops=2 * rows_here * n_act * total * pairs,
            bytes_accessed=4 * rows_here * n_act * pairs,
            transcendentals=0,
        ),
    )(moved, pltpu.with_memory_space_constraint(density, pltpu.HBM))


def orb_partner(value, step):
    count = lax.axis_size("orb")
    return lax.ppermute(value, "orb", [(i, i ^ step) for i in range(count)])


def exchange_sum(value):
    step = 1
    while step < lax.axis_size("orb"):
        value = value + orb_partner(value, step)
        step *= 2
    return value


def packed_shards(cholesky, active_coeff, pair_density):
    vec_count = lax.axis_size("vec")
    orb_pos = lax.axis_index("orb")
    local_vecs, block_rows, _ = cholesky.shape
    n_act = active_coeff.shape[1]
    pairs = n_act * n_act
    half, partial_value = transform(cholesky, active_coeff.T, orb_pos)
    step = 1
    while 2 * step < lax.axis_size("orb"):
        partial_value = partial_value + orb_partner(partial_value, step)
        step *= 2
    other = orb_partner(partial_value, step)
    packed = pack(split(half, local_vecs), partial_value, other, local_vecs, n_act)
    order = [reverse(i, vec_count) for i in range(vec_count)]
    moved = lax.all_to_all(packed, "vec", 0, 0, axis_index_groups=[order], tiled=True)
    density = pair_density.reshape(pairs, pairs)
    integrals, fock = finish(moved, density, local_vecs, n_act)
    return (integrals, fock.T)


def plain_shards(cholesky, active_coeff, pair_density):
    vec_count = lax.axis_size("vec")
    orb_pos = lax.axis_index("orb")
    local_vecs, block_rows, _ = cholesky.shape
    n_act = active_coeff.shape[1]
    rows_here = block_rows // vec_count
    half = jnp.einsum("qmn,nu->mqu", cholesky, active_coeff, preferred_element_type=F32).astype(BF16)
    coeff_rows = lax.dynamic_slice_in_dim(active_coeff, orb_pos * block_rows, block_rows, 0)
    partial_value = jnp.einsum("mv,mqw->vqw", coeff_rows, half, preferred_element_type=F32)
    own = exchange_sum(partial_value.reshape(n_act, local_vecs * n_act)).astype(BF16)
    flat = half.reshape(vec_count, rows_here, local_vecs * n_act)
    packed = jnp.concatenate([flat, jnp.broadcast_to(own[None], (vec_count,) + own.shape)], axis=1)
    moved = lax.all_to_all(packed, "vec", split_axis=0, concat_axis=0, tiled=True)
    moved = moved.reshape(vec_count, rows_here + n_act, local_vecs, n_act)
    regrouped = moved[:, :rows_here]
    active = moved[:, rows_here:].transpose(0, 2, 1, 3).reshape(vec_count, local_vecs, n_act * n_act)
    integrals = jnp.einsum("smqu,sqx->mux", regrouped, active, preferred_element_type=F32)
    fock = jnp.dot(
        integrals.reshape(rows_here, -1),
        pair_density.astype(F32).reshape(n_act, -1).T,
        precision=lax.Precision.HIGHEST,
    )
    return (integrals, fock)


def shards(cholesky, active_coeff, pair_density):
    vecs, block_rows, basis = cholesky.shape
    n_act = active_coeff.shape[1]
    vec_count = lax.axis_size("vec")
    fits = (
        block_rows == vec_count * (LANES // 2)
        and vec_count % 16 == 0
        and vec_count & (vec_count - 1) == 0
        and lax.axis_size("orb") > 1
        and vecs % 2 == 0
        and vecs * n_act <= LANES
        and vecs * n_act % 16 == 0
        and n_act % SUBLANES == 0
    )
    body = packed_shards if fits else plain_shards
    return body(cholesky, active_coeff, pair_density)


def solution(mesh):
    return jax.shard_map(
        shards,
        mesh=mesh,
        in_specs=(P("vec", "orb", None), P(), P()),
        out_specs=(P(("orb", "vec"), None, None), P(("orb", "vec"), None)),
        check_vma=False,
    )
```

time: 70.4 us -> 31.1 us (0.44)
  blocking collectives: 44.7 us -> 18 us
  matrix products: 14.3 us -> 0 us
  Pallas kernels: 0 us -> 11.6 us
  starting transfers between devices: 8.31 us -> 0.52 us
  local copies, waits for them, and re-layouts: 2.18 us -> 0 us
    all_gather x1 -> x0, blocking collectives: 41.4 us -> none  [shards(): lax.all_gather(own_active, 'vec', axis=0, tiled=True)]
    all_to_all x0 -> x1, blocking collectives: none -> 18 us  [packed_shards(): lax.all_to_all(packed, 'vec', 0, 0, axis_index_groups=[order], tiled=True)]
    dot_general x4 -> x0, matrix products: 14.3 us -> none  [the longest x1 10.4 us: shards(): jnp.einsum('qmn,nu->mqu', cholesky, active_coeff, preferred_element_type=...]
    pallas_call x0 -> x4, Pallas kernels: none -> 11.6 us  [the longest x1 7.66 us: transform(): pl.pallas_call(transform_kernel, out_shape=(jax.ShapeDtypeStruct((block_r...]
    all_to_all x1 -> x0, starting transfers between devices: 8.31 us -> none  [shards(): moved = lax.all_to_all(flat, 'vec', split_axis=0, concat_axis=1, tiled=True)]
    psum x1 -> x0, blocking collectives: 3.3 us -> none  [shards(): own_sum = lax.psum(partial_value.reshape(local_vecs, n_act * n_act), 'orb')]
    all_to_all x3 -> x0, local copies, waits for them, and re-layouts: 1.57 us -> none  [shards(): moved = lax.all_to_all(flat, 'vec', split_axis=0, concat_axis=1, tiled=True)]
  transfers between devices with their start and end apart: 1 -> 1, of which waited for: 0 -> 1; matrix products, arithmetic and copies ran while one was open for 1% -> 0% of each run, Pallas kernels for 0% -> 2%
where the time goes in v1:
time: 31.1 us; the launch traced here: 30.9 us
  blocking collectives  18 us (58%)
  Pallas kernels  11.6 us (37%)
  between operations  0.66 us (2%)
  starting transfers between devices  0.52 us (2%)
    all_to_all x1, blocking collectives, packed_shards(): lax.all_to_all(packed, 'vec', 0, 0, axis_index_groups=[order], tiled=True)  18 us
    pallas_call x1, Pallas kernels, transform(): pl.pallas_call(transform_kernel, out_shape=(jax.ShapeDtypeStruct((block_r...  7.66 us
    pallas_call x1, Pallas kernels, finish(): pl.pallas_call(functools.partial(finish_kernel, vecs, n_act), out_shape=(...  2.96 us
    pallas_call x1, Pallas kernels, split(): pl.pallas_call(functools.partial(chunk_kernel, vecs), out_shape=jax.Shape...  0.7 us
  transfers between devices with their start and end apart: 1, of which 1 were waited for; matrix products, arithmetic and copies ran while one was open for 0% of the time, Pallas kernels for 2%

profile of v1, /device:TPU:0, one launch (start us, length us, event | category | flops | bytes accessed | tf_op | source)
XLA Modules:
  0.0 30.9 jit_solution(909261648558578729)
XLA Ops:
  0.6 7.7 %shard_map.50 = (f32[8,96,128]{2,1,0:T(8,128)S(1)}, f32[24,96]{1,0:T(8,128)S(1)}) custom-call(s32[1]{0:T(128)} %bitcast.orb_ref, bf16[4096,2048]{1,0:T(8,128)(2,1)} %bitcast.5, bf16[24,2048]{1,0:T(8,128)(2,1)} %bitcast.7), custom_call_target="tpu_custom_call" | custom-call | flops 4294967296 | bytes 16777216 | tf_op jit(solution)/shard_map/pallas_call | solution.py:84
  8.3 0.5 %collective-permute-start = (f32[24,96]{1,0:T(8,128)S(1)}, f32[24,96]{1,0:T(8,128)S(1)}, u32[]{:S(2)}, u32[]{:S(2)}) collective-permute-start(f32[24,96]{1,0:T(8,128)S(1)} %get-tuple-element.7.own_ref), channel_id=1, source_target_pairs={{0,1},{1,0},{2,3},{3,2},{4,5},{5,4},{6,7},{7,6},{8,9},{9,8},{10,11... | collective-permute-start | bytes 27656 | tf_op jit(solution)/shard_map/ppermute | solution.py:314
  8.8 0.7 %shard_map.51.packed_in = bf16[16,4,2176]{2,1,0:T(4,128)(2,1)S(1)} custom-call(f32[8,96,128]{2,1,0:T(8,128)S(1)} %get-tuple-element.6.half_ref), custom_call_target="tpu_custom_call" | custom-call | bytes 1048576 | tf_op jit(solution)/shard_map/pallas_call | solution.py:157
  9.5 0.1 collective-permute-done.other_ref
  9.6 0.2 shard_map.52
  9.9 18.0 %all_to_all.5.moved_ref = bf16[16,4,2176]{2,1,0:T(4,128)(2,1)S(1)} all-to-all(bf16[16,4,2176]{2,1,0:T(4,128)(2,1)S(1)} %shard_map.52), channel_id=1, replica_groups={{0,16,8,24,4,20,12,28,2,18,10,26,6,22,14,30},{1,17,9,25,5,21,13,29,3,19..., dimensions={0} | all-to-all | bytes 557056 | tf_op jit(solution)/shard_map/all_to_all | solution.py:339
  27.9 3.0 %shard_map.53 = (f32[64,24,576]{2,1,0:T(8,128)}, f32[24,64]{1,0:T(8,128)}) custom-call(bf16[16,4,2176]{2,1,0:T(4,128)(2,1)S(1)} %all_to_all.5.moved_ref, bf16[576,576]{1,0:T(8,128)(2,1)} %bitcast.6), custom_call_target="tpu_custom_call" | custom-call | flops 113246208 | bytes 3538944 | tf_op jit(solution)/shard_map/pallas_call | solution.py:280
Async XLA Ops:
  8.3 1.4 %collective-permute-start = (f32[24,96]{1,0:T(8,128)S(1)}, f32[24,96]{1,0:T(8,128)S(1)}, u32[]{:S(2)}, u32[]{:S(2)}) collective-permute-start(f32[24,96]{1,0:T(8,128)S(1)} %get-tuple-element.7.own_ref), channel_id=1, source_target_pairs={{0,1},{1,0},{2,3},{3,2},{4,5},{5,4},{6,7},{7,6},{8,9},{9,8},{10,11... | collective-permute-start | bytes 27656 | tf_op jit(solution)/shard_map/ppermute | solution.py:314
